TPU v7x, 32 devices: a whole 2x2x4 slice. The times are simulated.
32 devices in a mesh: groups: 2 (over x), isl: 16 (over z, y, core).
Axes of the slice: x: 2, y: 2, z: 4, core: 2. Of those that a mesh axis runs over, the one named last changes fastest.
Arguments:
- particles: bfloat16 [262144, 256], P(('groups', 'isl')), parts along dimension 0, may hold values from -6 to 6
- noise: bfloat16 [3, 262144, 256], P(None, ('groups', 'isl')), parts along dimension 1, may hold values from -3 to 3
- series: float32 [6, 256], P('groups'), parts along dimension 0, may hold values from -6 to 6
- transition: bfloat16 [256, 256], replicated, may hold values from -0.375 to 0.375
- obs_matrix: bfloat16 [256, 256], replicated, may hold values from -0.375 to 0.375
- precision: float32 [256], replicated, may hold values from 1 to 10
- src_island: int32 [3, 2048, 1], P(None, ('groups', 'isl')), parts along dimension 1, may hold values from 0 to 15; in each aligned block of 32 rows (0 to 31, 32 to 63, ..., all dimensions but the last counted through in order) at most 4 rows name the same one
- src_tile: int32 [3, 2048], P(None, ('groups', 'isl')), parts along dimension 1, may hold values from 0 to 63
- swap_bits: int32 [6], P('groups'), parts along dimension 0, may hold values from 0 to 3, as said below
Outputs:
- cloud: bfloat16 [262144, 256], P(('groups', 'isl')), parts along dimension 0
- first_moment: float32 [6, 256], P('groups'), parts along dimension 0
- second_moment: float32 [6, 256, 256], P('groups', 'isl'), parts along dimension 0
There are 2 independent parts, one for each index of `groups`. A program takes and returns all parts, laid end to end along the dimension named above; an argument that names none is the same for every part. Nothing has to cross between parts.
Inputs may be any that keep to these rules, and one draw needn't show every extreme that they name: `src_island`: within each aligned block of 32 slots (half of one island's slots), no island is named more than 4 times; some island is named exactly that often. `swap_bits`: bits lie below log2(16); the top one occurs in every draw.
All inputs are finite; a program needn't handle non-finite values.
Results may differ from a plain program's by a relative error of at most 0.0085.
Values may be sent and summed in bfloat16 or wider, within the bound.
A program may use at most 128 MiB of HBM per device.

v0:
```python
import jax
import jax.numpy as jnp
from jax import lax
from jax.sharding import PartitionSpec as P

TILE = 128
STEPS = 3


def plan_slots(island_table, tile_table, own_index, capacity, islands):
    matches = (island_table == own_index).astype(jnp.int32)
    position = jnp.cumsum(matches, axis=1) - 1
    chosen = (matches[:, :, None] > 0) & (
        position[:, :, None] == jnp.arange(capacity, dtype=jnp.int32)[None, None, :]
    )
    send_tile = jnp.sum(jnp.where(chosen, tile_table[:, :, None], 0), axis=1)
    own_sources = lax.dynamic_index_in_dim(island_table, own_index, 0, keepdims=False)
    source_onehot = (own_sources[:, None] == jnp.arange(islands, dtype=jnp.int32)[None, :]).astype(
        jnp.int32
    )
    own_position = jnp.sum((jnp.cumsum(source_onehot, axis=0) - 1) * source_onehot, axis=1)
    return (send_tile, own_sources * capacity + own_position)


def local(
    particles, noise, series, transition, obs_matrix, precision, src_island, src_tile, swap_bits
):
    islands = lax.axis_size("isl")
    own_index = lax.axis_index("isl")
    row_count = particles.shape[0]
    width = particles.shape[1]
    tile_rows = TILE
    tile_count = row_count // tile_rows
    halfway = tile_count // 2
    half_capacity = max(2, tile_count // islands)
    capacity = 2 * half_capacity
    all_islands, all_tiles = (
        lax.all_gather(src_island[:, :, 0], "isl", axis=1, tiled=True),
        lax.all_gather(src_tile, "isl", axis=1, tiled=True),
    )
    cloud = particles
    firsts = []
    seconds = []
    for step in range(STEPS):
        propagated = (
            jnp.dot(cloud, transition, preferred_element_type=jnp.float32)
            + noise[step].astype(jnp.float32)
        ).astype(jnp.bfloat16)
        predicted = jnp.dot(propagated, obs_matrix, preferred_element_type=jnp.float32)
        innovation = series[step][None, :] - predicted
        likelihood = jnp.exp(-0.5 * jnp.mean(innovation * innovation * precision[None, :], axis=1))
        local_total = jnp.sum(likelihood)
        first_sums = jnp.sum(propagated.astype(jnp.float32) * likelihood[:, None], axis=0)
        weighted = (propagated.astype(jnp.float32) * likelihood[:, None]).astype(jnp.bfloat16)
        second_sums = lax.psum_scatter(
            jnp.dot(weighted.T, propagated, preferred_element_type=jnp.float32).astype(
                jnp.bfloat16
            ),
            "isl",
            scatter_dimension=0,
            tiled=True,
        ).astype(jnp.float32)
        weight_total, first_total = lax.psum((local_total, first_sums), "isl")
        firsts.append(first_total / weight_total)
        seconds.append(second_sums / weight_total)
        island_table = all_islands[step].reshape(islands, tile_count)
        tile_table = all_tiles[step].reshape(islands, tile_count)
        bit_value = jnp.left_shift(jnp.int32(1), swap_bits[step])
        partner_order = jnp.bitwise_xor(jnp.arange(islands, dtype=jnp.int32), bit_value)
        island_table = jnp.concatenate(
            [island_table[:, :halfway], island_table[partner_order, halfway:]], axis=1
        )
        tile_table = jnp.concatenate(
            [tile_table[:, :halfway], tile_table[partner_order, halfway:]], axis=1
        )
        tiles = propagated.reshape(tile_count, tile_rows, width)
        send_tile, receive_slot = plan_slots(island_table, tile_table, own_index, capacity, islands)
        incoming = lax.all_to_all(tiles[send_tile], "isl", split_axis=0, concat_axis=0, tiled=True)
        resampled = incoming.reshape(islands * capacity, tile_rows, width)[receive_slot]
        cloud = resampled.reshape(row_count, width)
    first_moment = jnp.stack(firsts)
    second_moment = jnp.stack(seconds)
    return (cloud, first_moment, second_moment)


def solution(mesh):
    return jax.shard_map(
        local,
        mesh=mesh,
        in_specs=(
            P(("groups", "isl"), None),
            P(None, ("groups", "isl"), None),
            P("groups", None),
            P(),
            P(),
            P(),
            P(None, ("groups", "isl"), None),
            P(None, ("groups", "isl")),
            P("groups"),
        ),
        out_specs=(P(("groups", "isl"), None), P("groups", None), P("groups", "isl", None)),
        check_vma=False,
    )
```

profile of v0, /device:TPU:13, one launch (start us, length us, event | category | flops | bytes accessed | tf_op | source)
XLA Modules:
  0.0 899.9 jit_solution(2495918141787877930)
XLA Ops:
  10.0 15.9 %all-gather.1 = s32[16,64,3]{1,2,0:T(4,128)S(1)} all-gather(s32[1,64,3]{1,2,0:T(4,128)} %bitcast.166), channel_id=1, replica_groups=mesh['groups'=2,'isl'=16] {'isl'}, dimensions={0}, use_global_device_ids=true | all-gather | bytes 13056 | tf_op jit(solution)/shard_map/all_gather | solution.py:39
  26.1 30.5 %while.7 = (s32[]{:T(128)}, s32[16,64]{1,0:T(8,128)S(1)}, s32[16,2]{0,1:T(2,128)S(1)}, s32[16,32]{1,0:T(8,128)S(1)}, s32[]{:T(128)}, /*index=5*/s32[]{:T(128)}) while((s32[]{:T(128)}, s32[16,64]{1,0:T(8,128)S(1)}, s32[16,2]{0,1:T(2,128)S(1)}, s32[16,32]{1,0:T(8,128)S(1)}, s32[]{:T(128)}, /*index=5*/s32[]{:T(128)}) %tuple.109), condition=%wide.while_cond.1, body=%wide.while_body.1.sunk | while | flops 2 | bytes 633 | solution.py:74
  56.6 22.8 %all-gather = s32[3,1024,1]{0,2,1:T(1,128)S(1)} all-gather(s32[3,64,1]{0,2,1:T(1,128)S(1)} %copy.29), channel_id=2, replica_groups=mesh['groups'=2,'isl'=16] {'isl'}, dimensions={1}, use_global_device_ids=true | all-gather | bytes 13056 | tf_op jit(solution)/shard_map/all_gather | solution.py:38
  79.4 57.8 %slice_reduce_fusion = (s32[1024]{0:T(1024)S(1)}, s32[1024]{0:T(1024)S(1)}, s32[1024]{0:T(1024)S(1)}) fusion(s32[3,1024,1]{0,2,1:T(1,128)S(1)} %all-gather), kind=kLoop, calls=%fused_computation.48 | loop fusion | bytes 24576 | tf_op jit(solution)/shard_map/slice | solution.py:66
  137.3 31.9 %while.6 = (s32[]{:T(128)}, s32[16,64]{1,0:T(8,128)S(1)}, s32[16,2]{0,1:T(2,128)S(1)}, s32[16,32]{1,0:T(8,128)S(1)}, s32[]{:T(128)}, /*index=5*/s32[]{:T(128)}) while((s32[]{:T(128)}, s32[16,64]{1,0:T(8,128)S(1)}, s32[16,2]{0,1:T(2,128)S(1)}, s32[16,32]{1,0:T(8,128)S(1)}, s32[]{:T(128)}, /*index=5*/s32[]{:T(128)}) %tuple.135), condition=%wide.while_cond, body=%wide.while_body.sunk | while | flops 2 | bytes 633 | solution.py:71
  170.2 6.7 fusion.6
  176.9 8.6 gather_fusion
  185.5 7.5 all-to-all-start
  194.4 30.5 %while.8 = (s32[]{:T(128)}, s32[16,64]{1,0:T(8,128)S(1)}, s32[16,2]{0,1:T(2,128)S(1)}, s32[16,32]{1,0:T(8,128)S(1)}, s32[]{:T(128)}, /*index=5*/s32[]{:T(128)}) while((s32[]{:T(128)}, s32[16,64]{1,0:T(8,128)S(1)}, s32[16,2]{0,1:T(2,128)S(1)}, s32[16,32]{1,0:T(8,128)S(1)}, s32[]{:T(128)}, /*index=5*/s32[]{:T(128)}) %tuple.118), condition=%wide.while_cond.2, body=%wide.while_body.2.sunk | while | flops 2 | bytes 633 | solution.py:71
  225.2 30.5 %while.9 = (s32[]{:T(128)}, s32[16,64]{1,0:T(8,128)S(1)}, s32[16,2]{0,1:T(2,128)S(1)}, s32[16,32]{1,0:T(8,128)S(1)}, s32[]{:T(128)}, /*index=5*/s32[]{:T(128)}) while((s32[]{:T(128)}, s32[16,64]{1,0:T(8,128)S(1)}, s32[16,2]{0,1:T(2,128)S(1)}, s32[16,32]{1,0:T(8,128)S(1)}, s32[]{:T(128)}, /*index=5*/s32[]{:T(128)}) %tuple.134), condition=%wide.while_cond.3, body=%wide.while_body.3.sunk | while | flops 2 | bytes 633 | solution.py:74
  256.9 118.3 %all-to-all-done = bf16[16,8,128,256]{3,2,1,0:T(8,128)(2,1)} async-done(((bf16[16,8,128,256]{3,2,1,0:T(8,128)(2,1)}), bf16[16,8,128,256]{3,2,1,0:T(8,128)(2,1)}, u32[]{:S(2)}, u32[]{:S(2)}) %all-to-all-start) | async-done | bytes 8388640 | tf_op jit(solution)/shard_map/all_to_all | solution.py:78
  375.2 6.2 gather_fusion.1
  381.4 6.6 fusion.7
  388.1 8.6 gather_fusion.2
  396.6 4.8 all-to-all-start.1
  401.6 31.3 %while.10 = (s32[]{:T(128)}, s32[16,64]{1,0:T(8,128)S(1)}, s32[16,2]{0,1:T(2,128)S(1)}, s32[16,32]{1,0:T(8,128)S(1)}, s32[]{:T(128)}, /*index=5*/s32[]{:T(128)}) while((s32[]{:T(128)}, s32[16,64]{1,0:T(8,128)S(1)}, s32[16,2]{0,1:T(2,128)S(1)}, s32[16,32]{1,0:T(8,128)S(1)}, s32[]{:T(128)}, /*index=5*/s32[]{:T(128)}) %tuple.124), condition=%wide.while_cond.4, body=%wide.while_body.4.sunk | while | flops 2 | bytes 633 | solution.py:71
  433.2 31.8 %while.11 = (s32[]{:T(128)}, s32[16,64]{1,0:T(8,128)S(1)}, s32[16,2]{0,1:T(2,128)S(1)}, s32[16,32]{1,0:T(8,128)S(1)}, s32[]{:T(128)}, /*index=5*/s32[]{:T(128)}) while((s32[]{:T(128)}, s32[16,64]{1,0:T(8,128)S(1)}, s32[16,2]{0,1:T(2,128)S(1)}, s32[16,32]{1,0:T(8,128)S(1)}, s32[]{:T(128)}, /*index=5*/s32[]{:T(128)}) %tuple.133), condition=%wide.while_cond.5, body=%wide.while_body.5.sunk | while | flops 2 | bytes 633 | solution.py:74
  466.1 117.7 %all-to-all-done.1 = bf16[16,8,128,256]{3,2,1,0:T(8,128)(2,1)} async-done(((bf16[16,8,128,256]{3,2,1,0:T(8,128)(2,1)}), bf16[16,8,128,256]{3,2,1,0:T(8,128)(2,1)}, u32[]{:S(2)}, u32[]{:S(2)}) %all-to-all-start.1) | async-done | bytes 8388640 | tf_op jit(solution)/shard_map/all_to_all | solution.py:78
  583.8 6.2 gather_fusion.3
  589.9 6.7 fusion.8
  596.6 8.6 gather_fusion.4
  605.2 5.0 all-to-all-start.2
  610.5 3.8 fusion.24
  614.9 3.3 fusion.33
  621.6 3.8 fusion.25
  626.0 3.4 fusion.30
  632.6 3.8 fusion.26
  637.1 3.4 fusion.27
  643.3 168.2 %all-reduce.3 = (f32[256]{0:T(256)S(1)}, f32[]{:T(128)}, f32[256]{0:T(256)S(1)}, f32[]{:T(128)}, f32[256]{0:T(256)S(1)}, /*index=5*/f32[]{:T(128)}) all-reduce(f32[256]{0:T(256)S(1)} %fusion.10, f32[]{:T(128)} %get-tuple-element.133, f32[256]{0:T(256)S(1)} %fusion.12, ...), channel_id=1, replica_groups=mesh['groups'=2,'isl'=16] {'isl'}, use_global_device_ids=true, to_apply=%region_24.25 | all-reduce | flops 771 | bytes 6168 | tf_op jit(solution)/shard_map/psum | solution.py:63
  815.4 11.3 %reduce-scatter.6.cloned.1.call-done = bf16[16,256]{1,0:T(8,128)(2,1)} async-done(((bf16[256,256]{1,0:T(8,128)(2,1)}), bf16[16,256]{1,0:T(8,128)(2,1)}) %reduce-scatter.6.cloned.1.call-update) | async-done | bytes 8208 | tf_op jit(solution)/shard_map/reduce_scatter | solution.py:55
  828.0 56.9 %reduce-scatter.8.cloned.1.call-done = bf16[16,256]{1,0:T(8,128)(2,1)} async-done(((bf16[256,256]{1,0:T(8,128)(2,1)}), bf16[16,256]{1,0:T(8,128)(2,1)}) %reduce-scatter.8.cloned.1.call-update) | async-done | bytes 8208 | tf_op jit(solution)/shard_map/reduce_scatter | solution.py:55
  886.9 6.2 gather_fusion.5
  (492 shorter events, 211.4 us)
Async XLA Ops:
  7.2 163.0 %copy-start = (bf16[256,256]{1,0:T(8,128)(2,1)S(1)}, bf16[256,256]{1,0:T(8,128)(2,1)}, u32[]{:S(2)}) copy-start(bf16[256,256]{1,0:T(8,128)(2,1)} %param.12) | copy-start | bytes 393220
  185.5 189.7 %all-to-all-start = ((bf16[16,8,128,256]{3,2,1,0:T(8,128)(2,1)}), bf16[16,8,128,256]{3,2,1,0:T(8,128)(2,1)}, u32[]{:S(2)}, u32[]{:S(2)}) async-start(bf16[16,8,128,256]{3,2,1,0:T(8,128)(2,1)} %bitcast.141), calls=%async_computation | async-start | bytes 16777216 | tf_op jit(solution)/shard_map/all_to_all | solution.py:78
  396.6 187.1 %all-to-all-start.1 = ((bf16[16,8,128,256]{3,2,1,0:T(8,128)(2,1)}), bf16[16,8,128,256]{3,2,1,0:T(8,128)(2,1)}, u32[]{:S(2)}, u32[]{:S(2)}) async-start(bf16[16,8,128,256]{3,2,1,0:T(8,128)(2,1)} %bitcast.142), calls=%async_computation.1 | async-start | bytes 16777216 | tf_op jit(solution)/shard_map/all_to_all | solution.py:78
  605.2 5.2 copy-start.5
  605.2 5.3 copy-start.6
  605.2 5.3 copy-start.7
  605.2 281.7 %all-to-all-start.2 = ((bf16[16,8,128,256]{3,2,1,0:T(8,128)(2,1)}), bf16[16,8,128,256]{3,2,1,0:T(8,128)(2,1)}, u32[]{:S(2)}, u32[]{:S(2)}) async-start(bf16[16,8,128,256]{3,2,1,0:T(8,128)(2,1)} %bitcast.143), calls=%async_computation.2 | async-start | bytes 16777216 | tf_op jit(solution)/shard_map/all_to_all | solution.py:78
  610.2 203.9 %reduce-scatter.4.cloned.1.call-start = ((), (), s32[]{:S(2)}) async-start(), calls=%async_computation.6 | async-start | bytes 139264 | tf_op jit(solution)/shard_map/reduce_scatter | solution.py:55
  610.5 4.4 copy-start.2
  618.3 208.4 %reduce-scatter.6.cloned.1.call-start = ((), (), s32[]{:S(2)}) async-start(), calls=%async_computation.7 | async-start | bytes 139264 | tf_op jit(solution)/shard_map/reduce_scatter | solution.py:55
  621.6 4.4 copy-start.3
  629.4 255.4 %reduce-scatter.8.cloned.1.call-start = ((), (), s32[]{:S(2)}) async-start(), calls=%async_computation.8 | async-start | bytes 139264 | tf_op jit(solution)/shard_map/reduce_scatter | solution.py:55
  632.6 4.4 copy-start.4
  637.1 256.0 %copy-start.1 = (bf16[256,256]{1,0:T(8,128)(2,1)S(1)}, bf16[256,256]{1,0:T(8,128)(2,1)}, u32[]{:S(2)}) copy-start(bf16[256,256]{1,0:T(8,128)(2,1)} %param.12) | copy-start | bytes 393220
Sparse Core Ops, SparseCore 0:
  618.4 125.9 reduce-scatter.3
  747.8 78.8 reduce-scatter.5
  830.7 54.1 reduce-scatter.7
where the time goes:
time: 915 us; the launch traced here: 900 us
  waiting for transfers between devices  304 us (33%)
  local copies, waits for them, and re-layouts  292 us (32%)
  blocking collectives  207 us (23%)
  matrix products  41.5 us (5%)
  other arithmetic  21.2 us (2%)
  starting transfers between devices  17.9 us (2%)
  between operations  16.2 us (2%)
    all_to_all x3, waiting for transfers between devices, local(): lax.all_to_all(tiles[send_tile], 'isl', split_axis=0, concat_axis=0, tile...  236 us
    gather x384, local copies, waits for them, and re-layouts  186 us
    psum x1, blocking collectives, local(): weight_total, first_total = lax.psum((local_total, first_sums), 'isl')  168 us
    reduce_scatter x3, waiting for transfers between devices, local(): lax.psum_scatter(jnp.dot(weighted.T, propagated, preferred_element_type=j...  68.1 us
    slice x1, local copies, waits for them, and re-layouts, local(): island_table = all_islands[step].reshape(islands, tile_count)  57.8 us
    gather x3, local copies, waits for them, and re-layouts, local(): tiles[send_tile]  25.7 us
    all_gather x1, blocking collectives, local(): lax.all_gather(src_island[:, :, 0], 'isl', axis=1, tiled=True)  22.8 us
    dot_general x3, matrix products, local(): jnp.dot(cloud, transition, preferred_element_type=jnp.float32)  20.1 us
  transfers between devices with their start and end apart: 6, of which 4 were waited for; matrix products, arithmetic and copies ran while one was open for 18% of the time, Pallas kernels for 0%

commit v1 on v0

v1 whole, which is shorter than its diff:
```python
import functools

import jax
import jax.numpy as jnp
from jax import lax
from jax.experimental import pallas as pl
from jax.experimental.pallas import tpu as pltpu
from jax.sharding import PartitionSpec as P

TILE = 128
STEPS = 3
CHUNK = 8
MESH = pl.DeviceIdType.MESH


def exchange_kernel(islands, per_peer, *refs):
    count = len(per_peer)
    sources, targets = refs[:count], refs[count : 2 * count]
    send_sems, recv_sems, own_sems = refs[2 * count :]
    me = lax.axis_index("isl")
    barrier = pltpu.get_barrier_semaphore()

    def greet(k, carry):
        pl.semaphore_signal(
            barrier, inc=1, device_id={"isl": lax.rem(me + k, islands)}, device_id_type=MESH
        )
        return carry

    lax.fori_loop(1, islands, greet, 0)
    pl.semaphore_wait(barrier, islands - 1)

    def remote(a, k):
        peer = lax.rem(me + k, islands)
        return pltpu.make_async_remote_copy(
            src_ref=sources[a].at[peer] if per_peer[a] else sources[a],
            dst_ref=targets[a].at[me],
            send_sem=send_sems.at[a, k],
            recv_sem=recv_sems.at[a, k],
            device_id={"isl": peer},
            device_id_type=MESH,
        )

    def own(a):
        return pltpu.make_async_copy(
            sources[a].at[me] if per_peer[a] else sources[a], targets[a].at[me], own_sems.at[a]
        )

    def send(k, carry):
        for a in range(count):
            remote(a, k).start()
        return carry

    lax.fori_loop(1, islands, send, 0)
    for a in range(count):
        own(a).start()

    def finish(k, carry):
        for a in range(count):
            remote(a, k).wait()
        return carry

    lax.fori_loop(1, islands, finish, 0)
    for a in range(count):
        own(a).wait()


def exchange(arrays, per_peer, islands, collective_id, name):
    shapes = [
        jax.ShapeDtypeStruct(x.shape if each else (islands,) + x.shape, x.dtype)
        for x, each in zip(arrays, per_peer)
    ]
    count = len(arrays)
    return pl.pallas_call(
        functools.partial(exchange_kernel, islands, per_peer),
        out_shape=shapes,
        in_specs=[pl.BlockSpec(memory_space=pl.ANY)] * count,
        out_specs=[pl.BlockSpec(memory_space=pl.ANY)] * count,
        scratch_shapes=[
            pltpu.SemaphoreType.DMA((count, islands)),
            pltpu.SemaphoreType.DMA((count, islands)),
            pltpu.SemaphoreType.DMA((count,)),
        ],
        compiler_params=pltpu.CompilerParams(collective_id=collective_id, has_side_effects=True),
        name=name,
    )(*arrays)


def filter_kernel(slots, source_ref, send_ref, *refs):
    tiles = refs[:CHUNK]
    noise_ref, series_ref, transition_ref, obs_ref, precision_ref = refs[CHUNK : CHUNK + 5]
    packed_ref, second_ref, stats_ref, moved, sem = refs[CHUNK + 5 :]
    i = pl.program_id(0)
    width = transition_ref.shape[0]

    @pl.when(i == 0)
    def _():
        second_ref[...] = jnp.zeros_like(second_ref)
        stats_ref[...] = jnp.zeros_like(stats_ref)

    cloud = jnp.concatenate([t[0] for t in tiles], axis=0)
    propagated = (
        jnp.dot(cloud, transition_ref[...], preferred_element_type=jnp.float32)
        + noise_ref[0].astype(jnp.float32)
    ).astype(jnp.bfloat16)
    moved[pl.ds(i * CHUNK, CHUNK)] = propagated.reshape(CHUNK, TILE, width)
    innovation = series_ref[...] - jnp.dot(
        propagated, obs_ref[...], preferred_element_type=jnp.float32
    )
    misfit = jnp.mean(innovation * innovation * precision_ref[...], axis=1, keepdims=True)
    likelihood = jnp.exp(-0.5 * misfit)
    scaled = propagated.astype(jnp.float32) * likelihood
    stats_ref[0:1, :] += jnp.sum(scaled, axis=0, keepdims=True)
    stats_ref[1:2, :] += jnp.broadcast_to(jnp.sum(likelihood, axis=0, keepdims=True), (1, width))
    second_ref[...] += lax.dot_general(
        scaled.astype(jnp.bfloat16),
        propagated,
        (((0,), (0,)), ((), ())),
        preferred_element_type=jnp.float32,
    )

    @pl.when(i == pl.num_programs(0) - 1)
    def _():
        def pack(k, carry):
            pltpu.make_async_copy(moved.at[send_ref[k]], packed_ref.at[k], sem).start()
            return carry

        lax.fori_loop(0, slots, pack, 0, unroll=8)
        pltpu.make_async_copy(packed_ref, packed_ref, sem).wait()


def filter_step(
    step, tiles, source, send, noise, series, transition, obs_matrix, precision, tile_count
):
    width = transition.shape[0]
    slots = send.shape[0]
    rows = CHUNK * TILE
    whole = lambda i, *_: (0, 0)
    tile_specs = [
        pl.BlockSpec((1, TILE, width), lambda i, source, send, t=t: (source[i * CHUNK + t], 0, 0))
        for t in range(CHUNK)
    ]
    matmuls = 3 * 2 * tile_count * TILE * width * width
    return pl.pallas_call(
        functools.partial(filter_kernel, slots),
        grid_spec=pltpu.PrefetchScalarGridSpec(
            num_scalar_prefetch=2,
            grid=(tile_count // CHUNK,),
            in_specs=tile_specs
            + [
                pl.BlockSpec((1, rows, width), lambda i, *_: (step, i, 0)),
                pl.BlockSpec((1, width), whole),
                pl.BlockSpec((width, width), whole),
                pl.BlockSpec((width, width), whole),
                pl.BlockSpec((1, width), whole),
            ],
            out_specs=[
                pl.BlockSpec(memory_space=pl.ANY),
                pl.BlockSpec((width, width), whole),
                pl.BlockSpec((8, width), whole),
            ],
            scratch_shapes=[
                pltpu.VMEM((tile_count, TILE, width), jnp.bfloat16),
                pltpu.SemaphoreType.DMA,
            ],
        ),
        out_shape=[
            jax.ShapeDtypeStruct((slots, TILE, width), jnp.bfloat16),
            jax.ShapeDtypeStruct((width, width), jnp.float32),
            jax.ShapeDtypeStruct((8, width), jnp.float32),
        ],
        compiler_params=pltpu.CompilerParams(vmem_limit_bytes=40 * 1024 * 1024),
        cost_estimate=pl.CostEstimate(
            flops=matmuls, bytes_accessed=5 * tile_count * TILE * width * 2, transcendentals=0
        ),
        name="filter_step",
    )(source, send, *([tiles] * CHUNK), noise, series, transition, obs_matrix, precision)


def place_kernel(source_ref, *refs):
    tiles, out_ref = refs[:CHUNK], refs[CHUNK]
    for t in range(CHUNK):
        out_ref[pl.ds(t * TILE, TILE), :] = tiles[t][0]


def place(tiles, source, tile_count):
    width = tiles.shape[2]
    return pl.pallas_call(
        place_kernel,
        grid_spec=pltpu.PrefetchScalarGridSpec(
            num_scalar_prefetch=1,
            grid=(tile_count // CHUNK,),
            in_specs=[
                pl.BlockSpec((1, TILE, width), lambda i, source, t=t: (source[i * CHUNK + t], 0, 0))
                for t in range(CHUNK)
            ],
            out_specs=pl.BlockSpec((CHUNK * TILE, width), lambda i, *_: (i, 0)),
        ),
        out_shape=jax.ShapeDtypeStruct((tile_count * TILE, width), tiles.dtype),
        compiler_params=pltpu.CompilerParams(vmem_limit_bytes=16 * 1024 * 1024),
        name="place_tiles",
    )(source, *([tiles] * CHUNK))


def plan(parents, swap_bits, own_index, capacity, islands, tile_count):
    halfway = tile_count // 2
    upper = parents[:, :, halfway:]
    swapped = upper
    for bit in range(max(islands.bit_length() - 1, 1)):
        span = 1 << bit
        if 2 * span > islands:
            break
        flipped = upper.reshape(STEPS, islands // (2 * span), 2, span, halfway)[:, :, ::-1]
        swapped = jnp.where(
            (swap_bits == bit)[:, None, None], flipped.reshape(upper.shape), swapped
        )
    wanted = jnp.concatenate([parents[:, :, :halfway], swapped], axis=2)
    island, tile = wanted // tile_count, wanted % tile_count
    before = jnp.arange(tile_count)[:, None] < jnp.arange(tile_count)[None, :]
    matches = island == own_index
    position = jnp.dot(
        matches.astype(jnp.bfloat16).reshape(STEPS * islands, tile_count),
        before.astype(jnp.bfloat16),
        preferred_element_type=jnp.float32,
    ).reshape(matches.shape)
    ranks = jnp.arange(capacity, dtype=jnp.float32)
    chosen = matches[:, :, None, :] & (position[:, :, None, :] == ranks[None, None, :, None])
    send = jnp.sum(jnp.where(chosen, tile[:, :, None, :], 0), axis=3)
    own = lax.dynamic_index_in_dim(island, own_index, 1, keepdims=False)
    same = (own[:, :, None] == own[:, None, :]) & before[None]
    source = own * capacity + jnp.sum(same.astype(jnp.int32), axis=1)
    return send.reshape(STEPS, islands * capacity), source


def local(
    particles, noise, series, transition, obs_matrix, precision, src_island, src_tile, swap_bits
):
    islands = lax.axis_size("isl")
    own_index = lax.axis_index("isl")
    row_count, width = particles.shape
    tile_count = row_count // TILE
    half_capacity = max(2, tile_count // islands)
    capacity = 2 * half_capacity
    table = src_island[:, :, 0] * tile_count + src_tile
    table = jnp.pad(table, ((0, 8 - STEPS), (0, 128 - tile_count)))
    (tables,) = exchange([table], [False], islands, 0, "share_tables")
    parents = jnp.swapaxes(tables[:, :STEPS, :tile_count], 0, 1)
    send, source = plan(parents, swap_bits, own_index, capacity, islands, tile_count)
    tiles = particles.reshape(tile_count, TILE, width)
    slot = jnp.arange(tile_count, dtype=jnp.int32)
    band = width // islands
    firsts, seconds = [], []
    for step in range(STEPS):
        packed, second, stats = filter_step(
            step,
            tiles,
            slot,
            send[step],
            noise,
            series[step : step + 1],
            transition,
            obs_matrix,
            precision[None, :],
            tile_count,
        )
        incoming, bands, all_stats = exchange(
            [
                packed.reshape(islands, capacity * TILE, width),
                second.reshape(islands, band, width),
                stats,
            ],
            [True, True, False],
            islands,
            1,
            "exchange_tiles",
        )
        tiles = incoming.reshape(islands * capacity, TILE, width)
        slot = source[step]
        total = jnp.sum(all_stats, axis=0)
        firsts.append(total[0] / total[1, 0])
        seconds.append(jnp.sum(bands, axis=0) / total[1, 0])
    cloud = place(tiles, slot, tile_count)
    return (cloud, jnp.stack(firsts), jnp.stack(seconds))


def solution(mesh):
    return jax.shard_map(
        local,
        mesh=mesh,
        in_specs=(
            P(("groups", "isl"), None),
            P(None, ("groups", "isl"), None),
            P("groups", None),
            P(),
            P(),
            P(),
            P(None, ("groups", "isl"), None),
            P(None, ("groups", "isl")),
            P("groups"),
        ),
        out_specs=(P(("groups", "isl"), None), P("groups", None), P("groups", "isl", None)),
        check_vma=False,
    )
```

time: 915 us -> 700 us (0.77); the launches traced: 900 us -> 699 us
  Pallas kernels: 0 us -> 660 us
  waiting for transfers between devices: 304 us -> 0 us
  local copies, waits for them, and re-layouts: 292 us -> 25.9 us
  blocking collectives: 207 us -> 0 us
  matrix products: 41.5 us -> 0.13 us
  starting transfers between devices: 17.9 us -> 0 us
  between operations: 16.2 us -> 0.94 us
  other arithmetic: 21.2 us -> 11.8 us
    pallas_call x0 -> x8, Pallas kernels: none -> 660 us  [the longest x4 589 us: exchange(): pl.pallas_call(functools.partial(exchange_kernel, islands, per_peer), out...]
    all_to_all x3 -> x0, waiting for transfers between devices: 236 us -> none  [local(): lax.all_to_all(tiles[send_tile], 'isl', split_axis=0, concat_axis=0, tile...]
    gather x390 -> x0, local copies, waits for them, and re-layouts: 230 us -> none
    psum x1 -> x0, blocking collectives: 168 us -> none  [local(): weight_total, first_total = lax.psum((local_total, first_sums), 'isl')]
    reduce_scatter x3 -> x0, waiting for transfers between devices: 68.1 us -> none  [local(): lax.psum_scatter(jnp.dot(weighted.T, propagated, preferred_element_type=j...]
    slice x4 -> x6, local copies, waits for them, and re-layouts: 59.2 us -> 2.51 us  [the longest x3 1.62 us: local(): firsts.append(total[0] / total[1, 0])]
    dot_general x9 -> x1, matrix products: 41.5 us -> 0.13 us  [plan(): jnp.dot(matches.astype(jnp.bfloat16).reshape(STEPS * islands, tile_count)...]
    all_gather x2 -> x0, blocking collectives: 38.7 us -> none  [the longest x1 22.8 us: local(): lax.all_gather(src_island[:, :, 0], 'isl', axis=1, tiled=True)]
  transfers between devices with their start and end apart: 6 -> 0, of which waited for: 4 -> 0; matrix products, arithmetic and copies ran while one was open for 18% -> 0% of each run, Pallas kernels for 0% -> 0%
where the time goes in v1:
time: 700 us; the launch traced here: 699 us
  Pallas kernels  660 us (94%)
  local copies, waits for them, and re-layouts  25.9 us (4%)
  other arithmetic  11.8 us (2%)
    pallas_call x4, Pallas kernels, exchange(): pl.pallas_call(functools.partial(exchange_kernel, islands, per_peer), out...  589 us
    pallas_call x3, Pallas kernels, filter_step(): pl.pallas_call(functools.partial(filter_kernel, slots), grid_spec=pltpu.P...  66.5 us
    unnamed x38, local copies, waits for them, and re-layouts  21.6 us

profile of v1, /device:TPU:13, one launch (start us, length us, event | category | flops | bytes accessed | tf_op | source)
XLA Modules:
  0.0 698.7 jit_solution(16155586970913597568)
XLA Ops:
  0.6 0.7 bitcast_add_fusion
  1.9 0.7 broadcast_compare_fusion.5
  2.6 0.8 fusion.9
  3.4 7.7 %share_tables.1 = s32[16,8,128]{2,1,0:T(8,128)} custom-call(s32[8,128]{1,0:T(8,128)} %pad.4.refs_0_), custom_call_target="tpu_custom_call" | custom-call | tf_op jit(solution)/shard_map/share_tables/pallas_call | solution.py:73
  11.1 0.8 slice_bitcast_fusion
  12.7 0.9 select_reduce_fusion
  13.9 2.2 copy-done.1
  16.1 0.9 copy-done.5
  17.0 0.9 copy-done.7
  17.9 0.7 copy-done.12
  18.6 21.3 %filter_step.3 = (bf16[128,128,256]{2,1,0:T(8,128)(2,1)S(1)}, f32[256,256]{1,0:T(8,128)S(1)}, f32[8,256]{1,0:T(8,128)S(1)}) custom-call(s32[64]{0:T(128)S(1)} %iota.24.source_ref, s32[128]{0:T(128)S(1)} %squeeze.44.send_ref, bf16[64,128,256]{2,1,0:T(8,128)(2,1)S(1)} %bitcast.64, bf16[64,128,256]{2,1,0:T(8,128)(2,1)S(1)} %bitcast.65, ...), custom_call_target="tpu_custom_call" | custom-call | flops 3221225472 | bytes 20971520 | tf_op jit(solution)/shard_map/filter_step/pallas_call | solution.py:143
  39.9 3.2 copy-done.4
  43.2 0.7 copy-done.11
  44.5 194.4 %exchange_tiles.3 = (bf16[16,1024,256]{2,1,0:T(8,128)(2,1)}, f32[16,16,256]{2,1,0:T(8,128)}, f32[16,8,256]{2,1,0:T(8,128)}) custom-call(bf16[16,1024,256]{2,1,0:T(8,128)(2,1)} %bitcast.74, f32[16,16,256]{2,1,0:T(8,128)} %bitcast.77, f32[8,256]{1,0:T(8,128)} %copy-done.16), custom_call_target="tpu_custom_call" | custom-call | tf_op jit(solution)/shard_map/exchange_tiles/pallas_call | solution.py:73
  238.9 0.9 reduce_sum.74
  240.3 0.6 slice_divide_fusion.2
  241.0 1.0 reduce_sum.77
  242.0 0.7 divide_bitcast_fusion.2
  242.6 22.6 %filter_step.4 = (bf16[128,128,256]{2,1,0:T(8,128)(2,1)S(1)}, f32[256,256]{1,0:T(8,128)S(1)}, f32[8,256]{1,0:T(8,128)S(1)}) custom-call(s32[64]{0:T(128)S(1)} %get-tuple-element.49.source_ref, s32[128]{0:T(128)S(1)} %squeeze.43.send_ref, bf16[128,128,256]{2,1,0:T(8,128)(2,1)} %bitcast.81, bf16[128,128,256]{2,1,0:T(8,128)(2,1)} %bitcast.82, ...), custom_call_target="tpu_custom_call" | custom-call | flops 3221225472 | bytes 20971520 | tf_op jit(solution)/shard_map/filter_step/pallas_call | solution.py:143
  265.3 3.2 copy-done.2
  268.5 0.7 copy-done.9
  269.8 193.6 %exchange_tiles.4 = (bf16[16,1024,256]{2,1,0:T(8,128)(2,1)}, f32[16,16,256]{2,1,0:T(8,128)}, f32[16,8,256]{2,1,0:T(8,128)}) custom-call(bf16[16,1024,256]{2,1,0:T(8,128)(2,1)} %bitcast.72, f32[16,16,256]{2,1,0:T(8,128)} %bitcast.75, f32[8,256]{1,0:T(8,128)} %copy-done.14), custom_call_target="tpu_custom_call" | custom-call | tf_op jit(solution)/shard_map/exchange_tiles/pallas_call | solution.py:73
  463.4 0.9 reduce_sum.75
  464.9 1.0 reduce_sum.78
  465.9 22.6 %filter_step.5 = (bf16[128,128,256]{2,1,0:T(8,128)(2,1)S(1)}, f32[256,256]{1,0:T(8,128)S(1)}, f32[8,256]{1,0:T(8,128)S(1)}) custom-call(s32[64]{0:T(128)S(1)} %get-tuple-element.50.source_ref, s32[128]{0:T(128)S(1)} %squeeze.41.send_ref, bf16[128,128,256]{2,1,0:T(8,128)(2,1)} %bitcast.89, bf16[128,128,256]{2,1,0:T(8,128)(2,1)} %bitcast.90, ...), custom_call_target="tpu_custom_call" | custom-call | flops 3221225472 | bytes 20971520 | tf_op jit(solution)/shard_map/filter_step/pallas_call | solution.py:143
  488.5 3.2 copy-done.3
  491.8 0.7 copy-done.10
  493.1 193.7 %exchange_tiles.5 = (bf16[16,1024,256]{2,1,0:T(8,128)(2,1)}, f32[16,16,256]{2,1,0:T(8,128)}, f32[16,8,256]{2,1,0:T(8,128)}) custom-call(bf16[16,1024,256]{2,1,0:T(8,128)(2,1)} %bitcast.73, f32[16,16,256]{2,1,0:T(8,128)} %bitcast.76, f32[8,256]{1,0:T(8,128)} %copy-done.15), custom_call_target="tpu_custom_call" | custom-call | tf_op jit(solution)/shard_map/exchange_tiles/pallas_call | solution.py:73
  686.8 3.4 copy-done
  690.1 4.0 place_tiles.1
  694.8 1.3 slice_divide_fusion
  696.1 1.3 divide_bitcast_fusion
  (56 shorter events, 6.3 us)
Async XLA Ops:
  13.9 2.2 copy-start.1
  16.1 0.9 copy-start.5
  17.0 0.9 copy-start.7
  17.9 0.7 copy-start.12
  39.9 3.2 copy-start.4
  43.1 0.7 copy-start.11
  43.9 0.6 copy-start.16
  44.4 198.2 %copy-start.6 = (bf16[256,256]{1,0:T(8,128)(2,1)S(1)}, bf16[256,256]{1,0:T(8,128)(2,1)}, u32[]{:S(2)}) copy-start(bf16[256,256]{1,0:T(8,128)(2,1)} %refs_10_.5) | copy-start | bytes 393220
  44.5 198.2 %copy-start.8 = (bf16[256,256]{1,0:T(8,128)(2,1)S(1)}, bf16[256,256]{1,0:T(8,128)(2,1)}, u32[]{:S(2)}) copy-start(bf16[256,256]{1,0:T(8,128)(2,1)} %refs_11_.5) | copy-start | bytes 393220
  44.5 198.2 %copy-start.13 = (f32[256]{0:T(256)S(1)}, f32[256]{0:T(256)}, u32[]{:S(2)}) copy-start(f32[256]{0:T(256)} %param.14) | copy-start | bytes 3076
  265.3 3.2 copy-start.2
  268.5 0.7 copy-start.9
  269.2 0.6 copy-start.14
  488.5 3.2 copy-start.3
  491.8 0.7 copy-start.10
  492.5 0.6 copy-start.15
  686.8 3.4 copy-start
  690.1 4.1 copy-start.18
  690.1 4.6 copy-start.17
